TPU v7x, 1024 devices: a whole 4x4x32 slice. The times are simulated.
1024 devices in a mesh: blk: 64 (over y, z_lo), slab: 16 (over x, z_hi, core).
Axes of the slice: x: 4, y: 4, z: 32 (z_hi: 2, z_lo: 16; z = z_hi * 16 + z_lo), core: 2. Of those that a mesh axis runs over, the one named last changes fastest.
Arguments:
- photo_features: bfloat16 [262144, 1152], P(('blk', 'slab')), may hold values from -1 to 1
- text_features: bfloat16 [262144, 1152], P(('blk', 'slab')), may hold values from -1 to 1
- partner_displacement: int32 [64, 16], replicated, may hold values from 0 to 255
- multiplier_factor: float32 [], replicated, may hold values from 1 to 4
- additive_shift_term: float32 [], replicated, may hold values from -3 to -1
Outputs:
- photo_feature_derivative: float32 [262144, 1152], P(('blk', 'slab'))
- text_feature_derivative: float32 [262144, 1152], P(('blk', 'slab'))
All inputs are finite; a program needn't handle non-finite values.
Results may differ from a plain program's by a relative error of at most 0.0025.
Values may be sent and summed in bfloat16 or wider, within the bound.
A program may use at most 32 MiB of HBM per device.

v0:
```python
import jax
import jax.numpy as jnp
from jax import lax
from jax.sharding import PartitionSpec as P

STEPS = 4


def passed_along(value, axis, steps):
    count = lax.axis_size(axis)
    pairs = [(source, (source + steps) % count) for source in range(count)]
    return lax.ppermute(value, axis, pairs)


def pick_offset(partner_displacement, blk_index, slab_index):
    return lax.dynamic_slice(partner_displacement, (blk_index, slab_index), (1, 1))[0, 0]


def body(
    photo_features, text_features, partner_displacement, multiplier_factor, additive_shift_term
):
    count = photo_features.shape[0]
    incoming = passed_along(text_features, "slab", 1)
    position = lax.broadcasted_iota(jnp.int32, (count, count), 0)
    column = lax.broadcasted_iota(jnp.int32, (count, count), 1)
    blk_index = lax.axis_index("blk")
    slab_index = lax.axis_index("slab")
    own_offset = pick_offset(partner_displacement, blk_index, slab_index)
    target = (column == (position + own_offset) % count).astype(jnp.float32)
    current = incoming
    photo_derivative_total = jnp.zeros(photo_features.shape, jnp.float32)
    carried = photo_derivative_total
    for k in range(STEPS):
        if k > 0:
            current = passed_along(current, "blk", 1)
        similarity_matrix = (
            multiplier_factor
            * lax.dot_general(
                photo_features,
                current,
                (((1,), (1,)), ((), ())),
                preferred_element_type=jnp.float32,
            )
            + additive_shift_term
        )
        likely = jax.nn.sigmoid(similarity_matrix)
        if k == 0:
            likely = likely - target
        weight = likely.astype(jnp.bfloat16)
        forward = jnp.dot(weight, current, preferred_element_type=jnp.float32)
        backward = lax.dot_general(
            weight, photo_features, (((0,), (0,)), ((), ())), preferred_element_type=jnp.float32
        )
        forward, backward = (forward, backward)
        photo_derivative_total = photo_derivative_total + forward
        if k == 0:
            carried = backward
        else:
            carried = passed_along(carried, "blk", 1) + backward
    gathered = passed_along(carried, "blk", -(STEPS - 1))
    local_entries = passed_along(gathered, "slab", -1)
    return (multiplier_factor * photo_derivative_total, multiplier_factor * local_entries)


def solution(mesh):
    return jax.shard_map(
        body,
        mesh=mesh,
        in_specs=(P(("blk", "slab"), None), P(("blk", "slab"), None), P(), P(), P()),
        out_specs=(P(("blk", "slab"), None), P(("blk", "slab"), None)),
        check_vma=False,
    )
```

profile of v0, /device:TPU:1, one launch (start us, length us, event | category | flops | bytes accessed | tf_op | source)
XLA Modules:
  0.0 452.4 jit_solution(5373220617196737777)
XLA Ops:
  0.6 0.0 copy-start
  0.6 30.2 %collective-permute-start = (bf16[256,1152]{1,0:T(8,128)(2,1)}, bf16[256,1152]{1,0:T(8,128)(2,1)S(1)}, u32[]{:S(2)}, u32[]{:S(2)}) collective-permute-start(bf16[256,1152]{1,0:T(8,128)(2,1)} %param.6), channel_id=1, source_target_pairs={{0,1},{1,2},{2,3},{3,4},{4,5},{5,6},{6,7},{7,8},{8,9},{9,10},{10,1... | collective-permute-start | bytes 1769480 | tf_op jit(solution)/shard_map/ppermute | solution.py:12
  32.2 1.3 dynamic_slice.3
  33.4 0.7 compare_and_fusion
  34.1 0.7 compare_select_fusion
  34.8 3.4 collective-permute-done
  38.1 0.0 copy-done
  38.1 0.4 fusion.22
  38.6 0.4 fusion.28
  38.9 42.7 %collective-permute-start.4 = (f32[256,1152]{1,0:T(8,128)S(1)}, f32[256,1152]{1,0:T(8,128)S(1)}, u32[]{:S(2)}, u32[]{:S(2)}) collective-permute-start(f32[256,1152]{1,0:T(8,128)S(1)} %fusion.28), channel_id=1, source_target_pairs={{0,16},{16,32},{32,48},{48,64},{64,80},{80,96},{96,112},{112,128},... | collective-permute-start | bytes 3538952 | tf_op jit(solution)/shard_map/ppermute | solution.py:12
  81.7 1.9 collective-permute-start.1
  83.6 42.1 %collective-permute-done.1 = bf16[256,1152]{1,0:T(8,128)(2,1)S(1)} collective-permute-done((bf16[256,1152]{1,0:T(8,128)(2,1)S(1)}, bf16[256,1152]{1,0:T(8,128)(2,1)S(1)}, u32[]{:S(2)}, u32[]{:S(2)}) %collective-permute-start.1) | collective-permute-done | bytes 589856 | tf_op jit(solution)/shard_map/ppermute | solution.py:12
  125.7 0.4 fusion.23
  126.1 0.0 collective-permute-done.4
  126.1 0.4 convolution_add_fusion
  126.5 15.3 %collective-permute-start.5 = (f32[256,1152]{1,0:T(8,128)S(1)}, f32[256,1152]{1,0:T(8,128)S(1)}, u32[]{:S(2)}, u32[]{:S(2)}) collective-permute-start(f32[256,1152]{1,0:T(8,128)S(1)} %convolution_add_fusion), channel_id=1, source_target_pairs={{0,16},{16,32},{32,48},{48,64},{64,80},{80,96},{96,112},{112,128},... | collective-permute-start | bytes 3538952 | tf_op jit(solution)/shard_map/ppermute | solution.py:12
  141.8 20.5 %collective-permute-start.2 = (bf16[256,1152]{1,0:T(8,128)(2,1)S(1)}, bf16[256,1152]{1,0:T(8,128)(2,1)S(1)}, u32[]{:S(2)}, u32[]{:S(2)}) collective-permute-start(bf16[256,1152]{1,0:T(8,128)(2,1)S(1)} %collective-permute-done.1), channel_id=1, source_target_pairs={{0,16},{16,32},{32,48},{48,64},{64,80},{80,96},{96,112},{112,128},... | collective-permute-start | bytes 1769480 | tf_op jit(solution)/shard_map/ppermute | solution.py:12
  162.3 24.4 %collective-permute-done.2 = bf16[256,1152]{1,0:T(8,128)(2,1)S(1)} collective-permute-done((bf16[256,1152]{1,0:T(8,128)(2,1)S(1)}, bf16[256,1152]{1,0:T(8,128)(2,1)S(1)}, u32[]{:S(2)}, u32[]{:S(2)}) %collective-permute-start.2) | collective-permute-done | bytes 589856 | tf_op jit(solution)/shard_map/ppermute | solution.py:12
  186.7 0.4 fusion.24
  187.0 0.4 fusion.29
  187.4 0.0 collective-permute-done.5
  187.4 0.1 add.86
  187.6 13.7 %collective-permute-start.6 = (f32[256,1152]{1,0:T(8,128)S(1)}, f32[256,1152]{1,0:T(8,128)S(1)}, u32[]{:S(2)}, u32[]{:S(2)}) collective-permute-start(f32[256,1152]{1,0:T(8,128)S(1)} %add.86), channel_id=1, source_target_pairs={{0,16},{16,32},{32,48},{48,64},{64,80},{80,96},{96,112},{112,128},... | collective-permute-start | bytes 3538952 | tf_op jit(solution)/shard_map/ppermute | solution.py:12
  201.2 3.8 collective-permute-start.3
  205.0 42.2 %collective-permute-done.3 = bf16[256,1152]{1,0:T(8,128)(2,1)S(1)} collective-permute-done((bf16[256,1152]{1,0:T(8,128)(2,1)S(1)}, bf16[256,1152]{1,0:T(8,128)(2,1)S(1)}, u32[]{:S(2)}, u32[]{:S(2)}) %collective-permute-start.3) | collective-permute-done | bytes 589856 | tf_op jit(solution)/shard_map/ppermute | solution.py:12
  247.2 0.4 fusion.25
  247.6 0.4 fusion.30
  248.0 0.0 collective-permute-done.6
  248.0 0.1 add.87
  248.2 1.9 collective-permute-start.7
  250.1 165.4 %collective-permute-done.7 = f32[256,1152]{1,0:T(8,128)S(1)} collective-permute-done((f32[256,1152]{1,0:T(8,128)S(1)}, f32[256,1152]{1,0:T(8,128)S(1)}, u32[]{:S(2)}, u32[]{:S(2)}) %collective-permute-start.7) | collective-permute-done | bytes 1179680 | tf_op jit(solution)/shard_map/ppermute | solution.py:12
  415.4 5.2 %collective-permute-start.8 = (f32[256,1152]{1,0:T(8,128)S(1)}, f32[256,1152]{1,0:T(8,128)S(1)}, u32[]{:S(2)}, u32[]{:S(2)}) collective-permute-start(f32[256,1152]{1,0:T(8,128)S(1)} %collective-permute-done.7), channel_id=1, source_target_pairs={{0,15},{1,0},{2,1},{3,2},{4,3},{5,4},{6,5},{7,6},{8,7},{9,8},{10,9... | collective-permute-start | bytes 3538952 | tf_op jit(solution)/shard_map/ppermute | solution.py:12
  420.6 0.3 fusion.27
  421.0 0.3 convolution_add_fusion.3
  421.3 0.3 convolution_add_fusion.2
  421.7 1.4 fusion
  423.1 28.2 %collective-permute-done.8 = f32[256,1152]{1,0:T(8,128)S(1)} collective-permute-done((f32[256,1152]{1,0:T(8,128)S(1)}, f32[256,1152]{1,0:T(8,128)S(1)}, u32[]{:S(2)}, u32[]{:S(2)}) %collective-permute-start.8) | collective-permute-done | bytes 1179680 | tf_op jit(solution)/shard_map/ppermute | solution.py:12
  451.3 1.1 broadcast_multiply_fusion
Async XLA Ops:
  0.6 37.5 %copy-start = (bf16[256,1152]{1,0:T(8,128)(2,1)S(1)}, bf16[256,1152]{1,0:T(8,128)(2,1)}, u32[]{:S(2)}) copy-start(bf16[256,1152]{1,0:T(8,128)(2,1)} %param.5) | copy-start | bytes 1769476
  0.6 37.5 %collective-permute-start = (bf16[256,1152]{1,0:T(8,128)(2,1)}, bf16[256,1152]{1,0:T(8,128)(2,1)S(1)}, u32[]{:S(2)}, u32[]{:S(2)}) collective-permute-start(bf16[256,1152]{1,0:T(8,128)(2,1)} %param.6), channel_id=1, source_target_pairs={{0,1},{1,2},{2,3},{3,4},{4,5},{5,6},{6,7},{7,8},{8,9},{9,10},{10,1... | collective-permute-start | bytes 1769480 | tf_op jit(solution)/shard_map/ppermute | solution.py:12
  38.9 87.2 %collective-permute-start.4 = (f32[256,1152]{1,0:T(8,128)S(1)}, f32[256,1152]{1,0:T(8,128)S(1)}, u32[]{:S(2)}, u32[]{:S(2)}) collective-permute-start(f32[256,1152]{1,0:T(8,128)S(1)} %fusion.28), channel_id=1, source_target_pairs={{0,16},{16,32},{32,48},{48,64},{64,80},{80,96},{96,112},{112,128},... | collective-permute-start | bytes 3538952 | tf_op jit(solution)/shard_map/ppermute | solution.py:12
  81.7 44.0 %collective-permute-start.1 = (bf16[256,1152]{1,0:T(8,128)(2,1)S(1)}, bf16[256,1152]{1,0:T(8,128)(2,1)S(1)}, u32[]{:S(2)}, u32[]{:S(2)}) collective-permute-start(bf16[256,1152]{1,0:T(8,128)(2,1)S(1)} %collective-permute-done), channel_id=1, source_target_pairs={{0,16},{16,32},{32,48},{48,64},{64,80},{80,96},{96,112},{112,128},... | collective-permute-start | bytes 1769480 | tf_op jit(solution)/shard_map/ppermute | solution.py:12
  126.5 60.9 %collective-permute-start.5 = (f32[256,1152]{1,0:T(8,128)S(1)}, f32[256,1152]{1,0:T(8,128)S(1)}, u32[]{:S(2)}, u32[]{:S(2)}) collective-permute-start(f32[256,1152]{1,0:T(8,128)S(1)} %convolution_add_fusion), channel_id=1, source_target_pairs={{0,16},{16,32},{32,48},{48,64},{64,80},{80,96},{96,112},{112,128},... | collective-permute-start | bytes 3538952 | tf_op jit(solution)/shard_map/ppermute | solution.py:12
  141.8 44.9 %collective-permute-start.2 = (bf16[256,1152]{1,0:T(8,128)(2,1)S(1)}, bf16[256,1152]{1,0:T(8,128)(2,1)S(1)}, u32[]{:S(2)}, u32[]{:S(2)}) collective-permute-start(bf16[256,1152]{1,0:T(8,128)(2,1)S(1)} %collective-permute-done.1), channel_id=1, source_target_pairs={{0,16},{16,32},{32,48},{48,64},{64,80},{80,96},{96,112},{112,128},... | collective-permute-start | bytes 1769480 | tf_op jit(solution)/shard_map/ppermute | solution.py:12
  187.6 60.5 %collective-permute-start.6 = (f32[256,1152]{1,0:T(8,128)S(1)}, f32[256,1152]{1,0:T(8,128)S(1)}, u32[]{:S(2)}, u32[]{:S(2)}) collective-permute-start(f32[256,1152]{1,0:T(8,128)S(1)} %add.86), channel_id=1, source_target_pairs={{0,16},{16,32},{32,48},{48,64},{64,80},{80,96},{96,112},{112,128},... | collective-permute-start | bytes 3538952 | tf_op jit(solution)/shard_map/ppermute | solution.py:12
  201.2 46.0 %collective-permute-start.3 = (bf16[256,1152]{1,0:T(8,128)(2,1)S(1)}, bf16[256,1152]{1,0:T(8,128)(2,1)S(1)}, u32[]{:S(2)}, u32[]{:S(2)}) collective-permute-start(bf16[256,1152]{1,0:T(8,128)(2,1)S(1)} %collective-permute-done.2), channel_id=1, source_target_pairs={{0,16},{16,32},{32,48},{48,64},{64,80},{80,96},{96,112},{112,128},... | collective-permute-start | bytes 1769480 | tf_op jit(solution)/shard_map/ppermute | solution.py:12
  248.2 167.3 %collective-permute-start.7 = (f32[256,1152]{1,0:T(8,128)S(1)}, f32[256,1152]{1,0:T(8,128)S(1)}, u32[]{:S(2)}, u32[]{:S(2)}) collective-permute-start(f32[256,1152]{1,0:T(8,128)S(1)} %add.87), channel_id=1, source_target_pairs={{0,976},{16,992},{32,1008},{48,0},{64,16},{80,32},{96,48},{112,64}... | collective-permute-start | bytes 3538952 | tf_op jit(solution)/shard_map/ppermute | solution.py:12
  415.4 35.8 %collective-permute-start.8 = (f32[256,1152]{1,0:T(8,128)S(1)}, f32[256,1152]{1,0:T(8,128)S(1)}, u32[]{:S(2)}, u32[]{:S(2)}) collective-permute-start(f32[256,1152]{1,0:T(8,128)S(1)} %collective-permute-done.7), channel_id=1, source_target_pairs={{0,15},{1,0},{2,1},{3,2},{4,3},{5,4},{6,5},{7,6},{8,7},{9,8},{10,9... | collective-permute-start | bytes 3538952 | tf_op jit(solution)/shard_map/ppermute | solution.py:12
where the time goes:
time: 460 us; the launch traced here: 452 us
  waiting for transfers between devices  306 us (67%)
  starting transfers between devices  135 us (29%)
  matrix products  5.48 us (1%)
    ppermute x9, waiting for transfers between devices, passed_along(): return lax.ppermute(value, axis, pairs)  306 us
    ppermute x9, starting transfers between devices, passed_along(): return lax.ppermute(value, axis, pairs)  135 us
  transfers between devices with their start and end apart: 9, of which 6 were waited for; matrix products, arithmetic and copies ran while one was open for 2% of the time, Pallas kernels for 0%

commit v1 on v0

v1 whole, which is shorter than its diff:
```python
import functools

import jax
import jax.numpy as jnp
from jax import lax
from jax.experimental import pallas as pl
from jax.experimental.pallas import tpu as pltpu
from jax.sharding import PartitionSpec as P

MESH = pl.DeviceIdType.MESH
STEPS = 4
NX, NY, HALF = 4, 4, 16
RING = 2 * HALF
X0 = HALF - 1
K0 = HALF + STEPS - 1
SLOTS = K0 + STEPS
PARTS = 2


def device(x, y, z, core):
    x, y, z = (x + NX) % NX, (y + NY) % NY, (z + RING) % RING
    return {"blk": y * HALF + z % HALF, "slab": x * 4 + (z // HALF) * 2 + core}


def kernel(
    photo, text, shifts, factor, bias, photo_out, text_out,
    own, slots, totals, ring_send, ring_recv, near_send, near_recv, side_send, side_recv, first_send, local,
):
    blk, slab = lax.axis_index("blk"), lax.axis_index("slab")
    x, half, core = slab // 4, (slab // 2) % 2, slab % 2
    y, z_lo = blk // HALF, blk % HALF
    z = half * HALF + z_lo
    other = 1 - core
    s = 2 * core - 1
    u = jnp.where(core == 1, z_lo, HALF - 1 - z_lo)
    rows = own.shape[1]
    piece = rows // PARTS

    @pl.when(core == 0)
    def _():
        pltpu.make_async_copy(text, own.at[0], local.at[0]).start()
        pltpu.make_async_copy(photo, own.at[1], local.at[1]).start()

    @pl.when(core == 1)
    def _():
        pltpu.make_async_copy(photo, own.at[0], local.at[0]).start()
        pltpu.make_async_copy(text, own.at[1], local.at[1]).start()

    ahead = device(x, y, z + s, core)
    behind = device(x, y, z - s, core)
    partner = device(x, y, z, other)
    x_far = jnp.where(core == 0, x - (1 - half), x + half)

    def x_from(z_source):
        h = ((z_source + RING) % RING) // HALF
        return jnp.where(core == 0, x - h, x + (1 - h))

    inject = device(x_far, y, z - s, other)
    inject_from = device(x_from(z - s), y, z - s, other)
    around = device(x, y - s, half * HALF + (z_lo + s * (HALF - 3) + RING) % HALF, other)
    k_side = jnp.minimum(HALF - u, STEPS - 1)
    side = device(x_far, y + s, z + s * k_side, other)

    barrier = pltpu.get_barrier_semaphore()

    def greet(d):
        pl.semaphore_signal(barrier, inc=1, device_id=d, device_id_type=MESH)

    for d in (ahead, behind, partner, inject, inject_from):
        greet(d)

    @pl.when(u <= 2)
    def _():
        greet(around)

    @pl.when(u >= HALF - 3)
    def _():
        greet(side)

    @pl.when(u == HALF - 1)
    def _():
        for k in range(1, STEPS):
            greet(device(x_from(z + s * k), y + s, z + s * k, other))

    peers = 5 + jnp.where(u <= 2, 1, 0) + jnp.where(u >= HALF - 3, 1, 0) + jnp.where(u == HALF - 1, 3, 0)
    pl.semaphore_wait(barrier, peers)

    def remote(src, dst, send, recv, d):
        return pltpu.make_async_remote_copy(
            src_ref=src, dst_ref=dst, send_sem=send, recv_sem=recv, device_id=d, device_id_type=MESH
        )

    pltpu.make_async_copy(text, own.at[1], local.at[1]).wait()

    def part(ref, slot, q):
        return ref.at[slot, pl.ds(pl.multiple_of(q * piece, piece), piece)]

    def injected(q):
        return remote(part(own, 1, q), part(slots, 0, q), ring_send.at[X0, q], ring_recv.at[0, q], inject)

    def onward(j, q):
        return remote(part(slots, j, q), part(slots, j + 1, q), ring_send.at[j, q], ring_recv.at[j + 1, q], ahead)

    for q in range(PARTS):
        injected(q).start()

    pltpu.make_async_copy(text, own.at[0], local.at[0]).wait()
    to_partner = remote(own.at[0], slots.at[K0], first_send.at[0], near_recv.at[0], partner)
    to_around = remote(own.at[0], slots.at[K0 + 3], first_send.at[1], near_recv.at[3], around)
    to_side = remote(own.at[1], slots.at[X0 + k_side], first_send.at[2], side_recv.at[k_side], side)
    to_partner.start()
    is_around, is_side = u <= 2, u >= HALF - 3
    pl.when(is_around)(to_around.start)
    pl.when(is_side)(to_side.start)

    def near_on(k):
        return remote(slots.at[K0 + k], slots.at[K0 + k + 1], near_send.at[k], near_recv.at[k + 1], ahead)

    def near_back(k):
        return remote(slots.at[K0 + k], slots.at[K0 + k - 1], near_send.at[k], near_recv.at[k - 1], behind)

    def side_back(k):
        return remote(slots.at[X0 + k], slots.at[X0 + k + 1], side_send.at[k], side_recv.at[k + 1], behind)

    def near_arrived(k):
        remote(slots.at[K0 + k], slots.at[K0 + k], near_send.at[k], near_recv.at[k], ahead).wait_recv()

    def goes_on(k):
        return (u >= k) & (u < HALF - 1)

    def goes_back(k):
        return (u < k) & (u >= 1)

    def near_plain(k):
        @pl.when(u >= k)
        def _():
            near_arrived(k)

        pl.when(goes_on(k))(near_on(k).start)

    def near_last():
        near_arrived(3)
        pl.when(goes_back(3))(near_back(3).start)

    def near_wrapped(k):
        @pl.when(u < k)
        def _():
            near_arrived(k)

        if k == 2:
            pl.when(goes_back(k))(near_back(k).start)

    def side_goes(k):
        return u >= HALF - 3 + (3 - k)

    def side_step(k):
        @pl.when(side_goes(k))
        def _():
            remote(slots.at[X0 + k], slots.at[X0 + k], side_send.at[k], side_recv.at[k], ahead).wait_recv()

        if k < 3:
            pl.when(side_goes(k))(side_back(k).start)

    def ring_step(j):
        for q in range(PARTS):
            remote(part(slots, j, q), part(slots, j, q), ring_send.at[j, q], ring_recv.at[j, q], ahead).wait_recv()
            onward(j, q).start()

    def ring_steps(first, last):
        def step(j, carry):
            ring_step(j)
            return carry

        lax.fori_loop(first, last, step, 0)

    multiplier, shift = factor[0], bias[0]
    caption_side = lax.rem(slab + 1, 16)
    as_image = shifts[blk, slab]
    as_caption = rows - shifts[blk, caption_side]
    near_offset = jnp.where(core == 0, as_caption, as_image)
    far_offset = jnp.where(core == 0, as_image, as_caption)
    position = lax.broadcasted_iota(jnp.int32, (rows, rows), 0)
    column = lax.broadcasted_iota(jnp.int32, (rows, rows), 1)

    def task(role, k, slot, offset):
        block = slots[slot]
        similarity = multiplier * lax.dot_general(
            own[role], block, (((1,), (1,)), ((), ())), preferred_element_type=jnp.float32
        ) + shift
        likely = jax.nn.sigmoid(similarity)
        hit = jnp.where(column == lax.rem(position + offset, rows), 1.0, 0.0)
        likely = likely - hit * jnp.where(k == 0, 1.0, 0.0)
        weight = likely.astype(jnp.bfloat16)
        totals[role] += jnp.dot(weight, block, preferred_element_type=jnp.float32)

    def near_task(k):
        task(0, k, K0 + k, near_offset)

    def far_task(k):
        task(1, k, jnp.where(u + k < HALF, X0 - k, X0 + k), far_offset)

    totals[...] = jnp.zeros_like(totals)
    near_plain(0)
    ring_steps(0, 2)
    near_plain(1)
    ring_steps(2, 4)
    near_plain(2)
    ring_steps(4, 6)
    near_last()
    side_step(1)
    ring_steps(6, 7)
    near_wrapped(2)
    side_step(2)
    ring_steps(7, 8)
    near_wrapped(1)
    side_step(3)

    def near_loop(k, carry):
        ring_step(HALF // 2 + k)
        near_task(k)
        return carry

    lax.fori_loop(0, STEPS, near_loop, 0)

    @pl.when(core == 0)
    def _():
        pltpu.make_async_copy(totals.at[0], text_out, local.at[0]).start()

    @pl.when(core == 1)
    def _():
        pltpu.make_async_copy(totals.at[0], photo_out, local.at[0]).start()

    def far_loop(k, carry):
        j = X0 - 3 + k

        @pl.when(k < STEPS - 1)
        def _():
            ring_step(j)

        @pl.when(k == STEPS - 1)
        def _():
            for q in range(PARTS):
                remote(part(slots, X0, q), part(slots, X0, q), ring_send.at[X0, q], ring_recv.at[X0, q], ahead).wait_recv()

        far_task(STEPS - 1 - k)
        return carry

    lax.fori_loop(0, STEPS, far_loop, 0)

    @pl.when(core == 0)
    def _():
        pltpu.make_async_copy(totals.at[1], photo_out, local.at[1]).start()

    @pl.when(core == 1)
    def _():
        pltpu.make_async_copy(totals.at[1], text_out, local.at[1]).start()

    def sent(j, carry):
        for q in range(PARTS):
            onward(j, q).wait_send()
        return carry

    lax.fori_loop(0, X0, sent, 0)
    for q in range(PARTS):
        injected(q).wait_send()
    to_partner.wait_send()
    pl.when(is_around)(to_around.wait_send)
    pl.when(is_side)(to_side.wait_send)
    for k in range(3):
        pl.when(goes_on(k))(near_on(k).wait_send)
    for k in (2, 3):
        pl.when(goes_back(k))(near_back(k).wait_send)
    for k in (1, 2):
        pl.when(side_goes(k))(side_back(k).wait_send)
    for role in range(2):
        pltpu.make_async_copy(totals.at[role], photo_out, local.at[role]).wait()


def body(photo_features, text_features, partner_displacement, multiplier_factor, additive_shift_term):
    rows, width = photo_features.shape
    anywhere = pl.BlockSpec(memory_space=pl.ANY)
    scalars = pl.BlockSpec(memory_space=pltpu.SMEM)
    total = jax.ShapeDtypeStruct((rows, width), jnp.float32)
    photo, text = pl.pallas_call(
        kernel,
        out_shape=(total, total),
        in_specs=[anywhere, anywhere, scalars, scalars, scalars],
        out_specs=(anywhere, anywhere),
        scratch_shapes=[
            pltpu.VMEM((2, rows, width), jnp.bfloat16),
            pltpu.VMEM((SLOTS, rows, width), jnp.bfloat16),
            pltpu.VMEM((2, rows, width), jnp.float32),
            pltpu.SemaphoreType.DMA((HALF, PARTS)),
            pltpu.SemaphoreType.DMA((HALF, PARTS)),
            pltpu.SemaphoreType.DMA((STEPS,)),
            pltpu.SemaphoreType.DMA((STEPS,)),
            pltpu.SemaphoreType.DMA((STEPS,)),
            pltpu.SemaphoreType.DMA((STEPS,)),
            pltpu.SemaphoreType.DMA((3,)),
            pltpu.SemaphoreType.DMA((2,)),
        ],
        compiler_params=pltpu.CompilerParams(
            collective_id=0, has_side_effects=True, vmem_limit_bytes=40 * 2**20
        ),
        cost_estimate=pl.CostEstimate(
            flops=32 * rows * rows * width, bytes_accessed=12 * rows * width, transcendentals=8 * rows * rows
        ),
    )(
        photo_features, text_features, partner_displacement,
        multiplier_factor.reshape(1), additive_shift_term.reshape(1),
    )
    return multiplier_factor * photo, multiplier_factor * text


def solution(mesh):
    return jax.shard_map(
        body,
        mesh=mesh,
        in_specs=(P(("blk", "slab"), None), P(("blk", "slab"), None), P(), P(), P()),
        out_specs=(P(("blk", "slab"), None), P(("blk", "slab"), None)),
        check_vma=False,
    )
```

time: 460 us -> 192 us (0.42)
  the two profiles are of different devices: /device:TPU:1 before, /device:TPU:32 now
where the time goes in v1:
time: 192 us
  Pallas kernels  185 us (96%)
  local copies, waits for them, and re-layouts  2.91 us (2%)
  between operations  1.93 us (1%)
    pallas_call x1, Pallas kernels, body(): pl.pallas_call(kernel, out_shape=(total, total), in_specs=[anywhere, anyw...  185 us

profile of v1, /device:TPU:32, one launch (start us, length us, event | category | flops | bytes accessed | tf_op | source)
XLA Modules:
  0.0 191.9 jit_solution(17859666488635256626)
XLA Ops:
  1.9 0.8 copy.7.shifts
  2.7 0.0 copy-start
  2.7 1.1 copy-done
  3.8 0.0 copy-start.1
  3.8 1.1 copy-done.1
  4.8 185.5 %shard_map.68 = (f32[256,1152]{1,0:T(8,128)S(1)}, f32[256,1152]{1,0:T(8,128)S(1)}) custom-call(bf16[256,1152]{1,0:T(8,128)(2,1)S(1)} %copy-done, bf16[256,1152]{1,0:T(8,128)(2,1)S(1)} %copy-done.1, s32[64,16]{1,0:T(8,128)S(1)} %copy.7.shifts, f32[1]{0:T(128)} %bitcast.2.factor, f32[1]{0:T(128)} %bitcast.3.bias), custom_call_target="tpu_custom_call" | custom-call | flops 2415919104 | bytes 3538944 | tf_op jit(solution)/shard_map/pallas_call | solution.py:284
  190.3 1.6 broadcast_multiply_fusion
Async XLA Ops:
  2.7 1.1 copy-start
  3.8 1.1 copy-start.1

commit v2 on v1

--- a/solution.py
+++ b/solution.py
@@ -14,7 +14,8 @@
 X0 = HALF - 1
 K0 = HALF + STEPS - 1
 SLOTS = K0 + STEPS
-PARTS = 2
+LAST = HALF - 1
+PARTS = 4
 
 
 def device(x, y, z, core):
@@ -24,7 +25,8 @@
 
 def kernel(
     photo, text, shifts, factor, bias, photo_out, text_out,
-    own, slots, totals, ring_send, ring_recv, near_send, near_recv, side_send, side_recv, first_send, local,
+    own, slots, totals, sums, shift_rows, ring_send, ring_recv, near_send, near_recv, side_send, side_recv, first_send,
+    own_send, own_recv, sum_send, sum_recv, local,
 ):
     blk, slab = lax.axis_index("blk"), lax.axis_index("slab")
     x, half, core = slab // 4, (slab // 2) % 2, slab % 2
@@ -36,6 +38,8 @@
     rows = own.shape[1]
     piece = rows // PARTS
 
+    pltpu.make_async_copy(shifts, shift_rows, local.at[2]).start()
+
     @pl.when(core == 0)
     def _():
         pltpu.make_async_copy(text, own.at[0], local.at[0]).start()
@@ -126,20 +130,45 @@
         remote(slots.at[K0 + k], slots.at[K0 + k], near_send.at[k], near_recv.at[k], ahead).wait_recv()
 
     def goes_on(k):
-        return (u >= k) & (u < HALF - 1)
+        return (u >= k) & (u < LAST - 2)
+
+    def takes_blocks(k):
+        return (u >= k) & (u < LAST - 1) if k else u >= 0
+
+    def lends(k):
+        return (u == 2) | (u == 1) if k == 1 else u == 2
+
+    def lend(k):
+        place = jnp.where(u == 2, 1 + k, 3)
+        return remote(slots.at[K0 + k], own.at[place], own_send.at[k], own_recv.at[place], partner)
+
+    def sum_on(n):
+        return remote(sums.at[n], sums.at[2 + n], sum_send.at[n], sum_recv.at[n], ahead)
+
+    def own_arrived(place):
+        remote(own.at[place], own.at[place], own_send.at[1], own_recv.at[place], partner).wait_recv()
+
+    def sum_arrived(n):
+        remote(sums.at[2 + n], sums.at[2 + n], sum_send.at[n], sum_recv.at[n], ahead).wait_recv()
 
     def goes_back(k):
         return (u < k) & (u >= 1)
 
     def near_plain(k):
-        @pl.when(u >= k)
+        @pl.when(takes_blocks(k))
         def _():
             near_arrived(k)
 
-        pl.when(goes_on(k))(near_on(k).start)
-
-    def near_last():
-        near_arrived(3)
+        if k < 3:
+            pl.when(goes_on(k))(near_on(k).start)
+        if k in (1, 2):
+            pl.when(lends(k))(lend(k).start)
+
+    def near_direct():
+        @pl.when(u < 3)
+        def _():
+            near_arrived(3)
+
         pl.when(goes_back(3))(near_back(3).start)
 
     def near_wrapped(k):
@@ -166,86 +195,105 @@
             remote(part(slots, j, q), part(slots, j, q), ring_send.at[j, q], ring_recv.at[j, q], ahead).wait_recv()
             onward(j, q).start()
 
-    def ring_steps(first, last):
-        def step(j, carry):
-            ring_step(j)
-            return carry
-
-        lax.fori_loop(first, last, step, 0)
-
+    pltpu.make_async_copy(shifts, shift_rows, local.at[2]).wait()
     multiplier, shift = factor[0], bias[0]
-    caption_side = lax.rem(slab + 1, 16)
-    as_image = shifts[blk, slab]
-    as_caption = rows - shifts[blk, caption_side]
+    at_blk = lax.broadcasted_iota(jnp.int32, (1, shift_rows.shape[1]), 1) == blk
+
+    def shift_of(slab_index):
+        return jnp.sum(jnp.where(at_blk, shift_rows[pl.ds(slab_index, 1), :], 0), axis=1, keepdims=True)
+
+    as_image = shift_of(slab)
+    as_caption = rows - shift_of(lax.rem(slab + 1, 16))
     near_offset = jnp.where(core == 0, as_caption, as_image)
     far_offset = jnp.where(core == 0, as_image, as_caption)
-    position = lax.broadcasted_iota(jnp.int32, (rows, rows), 0)
-    column = lax.broadcasted_iota(jnp.int32, (rows, rows), 1)
-
-    def task(role, k, slot, offset):
-        block = slots[slot]
+
+    def task(role, k, block, offset, first=0):
         similarity = multiplier * lax.dot_general(
             own[role], block, (((1,), (1,)), ((), ())), preferred_element_type=jnp.float32
         ) + shift
         likely = jax.nn.sigmoid(similarity)
+        position = lax.broadcasted_iota(jnp.int32, likely.shape, 0)
+        column = lax.broadcasted_iota(jnp.int32, likely.shape, 1) + first
         hit = jnp.where(column == lax.rem(position + offset, rows), 1.0, 0.0)
         likely = likely - hit * jnp.where(k == 0, 1.0, 0.0)
         weight = likely.astype(jnp.bfloat16)
         totals[role] += jnp.dot(weight, block, preferred_element_type=jnp.float32)
 
-    def near_task(k):
-        task(0, k, K0 + k, near_offset)
-
-    def far_task(k):
-        task(1, k, jnp.where(u + k < HALF, X0 - k, X0 + k), far_offset)
-
     totals[...] = jnp.zeros_like(totals)
-    near_plain(0)
-    ring_steps(0, 2)
-    near_plain(1)
-    ring_steps(2, 4)
-    near_plain(2)
-    ring_steps(4, 6)
-    near_last()
-    side_step(1)
-    ring_steps(6, 7)
-    near_wrapped(2)
-    side_step(2)
-    ring_steps(7, 8)
-    near_wrapped(1)
-    side_step(3)
-
-    def near_loop(k, carry):
-        ring_step(HALF // 2 + k)
-        near_task(k)
+
+    def step(j, carry):
+        ring_step(j)
+
+        for first, action in (
+            (1, lambda: near_plain(0)),
+            (3, lambda: near_plain(1)),
+            (4, near_direct),
+            (4, lambda: side_step(1)),
+            (5, lambda: near_plain(2)),
+            (7, lambda: near_wrapped(2)),
+            (7, lambda: side_step(2)),
+            (8, lambda: near_plain(3)),
+            (10, lambda: near_wrapped(1)),
+            (10, lambda: side_step(3)),
+        ):
+            pl.when(j == first)(action)
+
+        @pl.when((u == LAST - 2) & (j >= 5) & (j <= 7))
+        def _():
+            pl.when(j == 5)(lambda: own_arrived(2))
+            pl.when(j == 7)(lambda: own_arrived(3))
+
+            for n in range(2):
+                @pl.when((j != 6) | (n == 0))
+                def _():
+                    task(jnp.where(j == 7, 3, 2), 1, slots[K0 + jnp.where(j == 6, 2, n)], near_offset)
+
+            for n in range(2):
+                @pl.when(j == 6 + n)
+                def _():
+                    sums[n] = totals[2 + n].astype(jnp.bfloat16)
+                    sum_on(n).start()
+
+        @pl.when((u == LAST - 1) & (j == 10))
+        def _():
+            own_arrived(3)
+            task(3, 1, slots[K0], near_offset)
+            sum_arrived(1)
+            sums[1] = (totals[3] + sums[3].astype(jnp.float32)).astype(jnp.bfloat16)
+            sum_on(1).start()
+            sum_arrived(0)
+            totals[0] += sums[2].astype(jnp.float32)
+
+        @pl.when((j == 8) | ((j >= 9) & (j <= 11) & (u < LAST - 1)))
+        def _():
+            k = jnp.where(j == 8, 0, jnp.where(j == 9, 2, jnp.where(j == 10, 3, 1)))
+            task(0, k, slots[K0 + k], near_offset)
+
+        @pl.when((u == LAST) & (j == 13))
+        def _():
+            sum_arrived(1)
+            totals[0] += sums[3].astype(jnp.float32)
+
+        @pl.when((j == 13) & (core == 0))
+        def _():
+            pltpu.make_async_copy(totals.at[0], text_out, local.at[0]).start()
+
+        @pl.when((j == 13) & (core == 1))
+        def _():
+            pltpu.make_async_copy(totals.at[0], photo_out, local.at[0]).start()
+
+        @pl.when(j >= X0 - 3)
+        def _():
+            k = X0 - j
+            task(1, k, slots[jnp.where(u + k < HALF, X0 - k, X0 + k)], far_offset)
+
         return carry
 
-    lax.fori_loop(0, STEPS, near_loop, 0)
-
-    @pl.when(core == 0)
-    def _():
-        pltpu.make_async_copy(totals.at[0], text_out, local.at[0]).start()
-
-    @pl.when(core == 1)
-    def _():
-        pltpu.make_async_copy(totals.at[0], photo_out, local.at[0]).start()
-
-    def far_loop(k, carry):
-        j = X0 - 3 + k
-
-        @pl.when(k < STEPS - 1)
-        def _():
-            ring_step(j)
-
-        @pl.when(k == STEPS - 1)
-        def _():
-            for q in range(PARTS):
-                remote(part(slots, X0, q), part(slots, X0, q), ring_send.at[X0, q], ring_recv.at[X0, q], ahead).wait_recv()
-
-        far_task(STEPS - 1 - k)
-        return carry
-
-    lax.fori_loop(0, STEPS, far_loop, 0)
+    lax.fori_loop(0, X0, step, 0)
+    for q in range(PARTS):
+        last = part(slots, X0, q)
+        remote(last, last, ring_send.at[X0, q], ring_recv.at[X0, q], ahead).wait_recv()
+        task(1, 0, slots[X0, q * piece : (q + 1) * piece], far_offset, q * piece)
 
     @pl.when(core == 0)
     def _():
@@ -272,6 +320,10 @@
         pl.when(goes_back(k))(near_back(k).wait_send)
     for k in (1, 2):
         pl.when(side_goes(k))(side_back(k).wait_send)
+    for k in (1, 2):
+        pl.when(lends(k))(lend(k).wait_send)
+    pl.when(u == LAST - 2)(sum_on(0).wait_send)
+    pl.when((u == LAST - 2) | (u == LAST - 1))(sum_on(1).wait_send)
     for role in range(2):
         pltpu.make_async_copy(totals.at[role], photo_out, local.at[role]).wait()
 
@@ -279,17 +331,20 @@
 def body(photo_features, text_features, partner_displacement, multiplier_factor, additive_shift_term):
     rows, width = photo_features.shape
     anywhere = pl.BlockSpec(memory_space=pl.ANY)
+    hbm = pl.BlockSpec(memory_space=pltpu.HBM)
     scalars = pl.BlockSpec(memory_space=pltpu.SMEM)
     total = jax.ShapeDtypeStruct((rows, width), jnp.float32)
     photo, text = pl.pallas_call(
         kernel,
         out_shape=(total, total),
-        in_specs=[anywhere, anywhere, scalars, scalars, scalars],
+        in_specs=[hbm, hbm, hbm, scalars, scalars],
         out_specs=(anywhere, anywhere),
         scratch_shapes=[
-            pltpu.VMEM((2, rows, width), jnp.bfloat16),
+            pltpu.VMEM((4, rows, width), jnp.bfloat16),
             pltpu.VMEM((SLOTS, rows, width), jnp.bfloat16),
-            pltpu.VMEM((2, rows, width), jnp.float32),
+            pltpu.VMEM((4, rows, width), jnp.float32),
+            pltpu.VMEM((4, rows, width), jnp.bfloat16),
+            pltpu.VMEM(partner_displacement.shape[::-1], jnp.int32),
             pltpu.SemaphoreType.DMA((HALF, PARTS)),
             pltpu.SemaphoreType.DMA((HALF, PARTS)),
             pltpu.SemaphoreType.DMA((STEPS,)),
@@ -297,7 +352,11 @@
             pltpu.SemaphoreType.DMA((STEPS,)),
             pltpu.SemaphoreType.DMA((STEPS,)),
             pltpu.SemaphoreType.DMA((3,)),
+            pltpu.SemaphoreType.DMA((STEPS,)),
+            pltpu.SemaphoreType.DMA((STEPS,)),
             pltpu.SemaphoreType.DMA((2,)),
+            pltpu.SemaphoreType.DMA((2,)),
+            pltpu.SemaphoreType.DMA((3,)),
         ],
         compiler_params=pltpu.CompilerParams(
             collective_id=0, has_side_effects=True, vmem_limit_bytes=40 * 2**20
@@ -306,7 +365,7 @@
             flops=32 * rows * rows * width, bytes_accessed=12 * rows * width, transcendentals=8 * rows * rows
         ),
     )(
-        photo_features, text_features, partner_displacement,
+        photo_features, text_features, partner_displacement.T,
         multiplier_factor.reshape(1), additive_shift_term.reshape(1),
     )
     return multiplier_factor * photo, multiplier_factor * text

time: 192 us -> 177 us (0.922)
  the two profiles are of different devices: /device:TPU:32 before, /device:TPU:1 now
where the time goes in v2:
time: 177 us; the launch traced here: 176 us
  Pallas kernels  170 us (96%)
  local copies, waits for them, and re-layouts  2.82 us (2%)
  between operations  1.94 us (1%)
    pallas_call x1, Pallas kernels, body(): pl.pallas_call(kernel, out_shape=(total, total), in_specs=[hbm, hbm, hbm,...  170 us

profile of v2, /device:TPU:1, one launch (start us, length us, event | category | flops | bytes accessed | tf_op | source)
XLA Modules:
  0.0 176.4 jit_solution(3923415258772645187)
XLA Ops:
  1.9 0.0 copy-start
  1.9 1.1 copy-done
  3.0 0.0 copy-start.1
  3.0 1.1 copy-done.1
  4.1 0.0 copy-start.2
  4.1 0.7 copy-done.2
  4.8 170.1 %shard_map.68 = (f32[256,1152]{1,0:T(8,128)S(1)}, f32[256,1152]{1,0:T(8,128)S(1)}) custom-call(bf16[256,1152]{1,0:T(8,128)(2,1)S(1)} %copy-done, bf16[256,1152]{1,0:T(8,128)(2,1)S(1)} %copy-done.1, s32[16,64]{1,0:T(8,128)S(1)} %bitcast.5, f32[1]{0:T(128)} %bitcast.3.factor, f32[1]{0:T(128)} %bitcast.4.bias), custom_call_target="tpu_custom_call" | custom-call | flops 2415919104 | bytes 3538944 | tf_op jit(solution)/shard_map/pallas_call | solution.py:337
  174.8 1.6 broadcast_multiply_fusion
Async XLA Ops:
  1.9 1.1 copy-start
  3.0 1.1 copy-start.1
  4.1 0.7 copy-start.2

commit v3 on v2

--- a/solution.py
+++ b/solution.py
@@ -159,10 +159,13 @@
         def _():
             near_arrived(k)
 
-        if k < 3:
+        if k < 2:
             pl.when(goes_on(k))(near_on(k).start)
         if k in (1, 2):
             pl.when(lends(k))(lend(k).start)
+
+    def near_third():
+        pl.when(goes_on(2))(near_on(2).start)
 
     def near_direct():
         @pl.when(u < 3)
@@ -228,13 +231,14 @@
             (1, lambda: near_plain(0)),
             (3, lambda: near_plain(1)),
             (4, near_direct),
-            (4, lambda: side_step(1)),
             (5, lambda: near_plain(2)),
+            (6, lambda: side_step(1)),
             (7, lambda: near_wrapped(2)),
-            (7, lambda: side_step(2)),
-            (8, lambda: near_plain(3)),
+            (9, lambda: side_step(2)),
             (10, lambda: near_wrapped(1)),
-            (10, lambda: side_step(3)),
+            (11, lambda: near_plain(3)),
+            (12, lambda: side_step(3)),
+            (8, near_third),
         ):
             pl.when(j == first)(action)
 
@@ -264,9 +268,9 @@
             sum_arrived(0)
             totals[0] += sums[2].astype(jnp.float32)
 
-        @pl.when((j == 8) | ((j >= 9) & (j <= 11) & (u < LAST - 1)))
-        def _():
-            k = jnp.where(j == 8, 0, jnp.where(j == 9, 2, jnp.where(j == 10, 3, 1)))
+        @pl.when((j == 8) | (((j == 9) | (j == 10) | (j == 11)) & (u < LAST - 1)))
+        def _():
+            k = jnp.where(j == 11, 3, jnp.where(j == 10, 1, jnp.where(j == 9, 2, 0)))
             task(0, k, slots[K0 + k], near_offset)
 
         @pl.when((u == LAST) & (j == 13))
@@ -274,11 +278,11 @@
             sum_arrived(1)
             totals[0] += sums[3].astype(jnp.float32)
 
-        @pl.when((j == 13) & (core == 0))
+        @pl.when((j == 14) & (core == 0))
         def _():
             pltpu.make_async_copy(totals.at[0], text_out, local.at[0]).start()
 
-        @pl.when((j == 13) & (core == 1))
+        @pl.when((j == 14) & (core == 1))
         def _():
             pltpu.make_async_copy(totals.at[0], photo_out, local.at[0]).start()
 
@@ -359,7 +363,7 @@
             pltpu.SemaphoreType.DMA((3,)),
         ],
         compiler_params=pltpu.CompilerParams(
-            collective_id=0, has_side_effects=True, vmem_limit_bytes=40 * 2**20
+            collective_id=0, has_side_effects=True, vmem_limit_bytes=56 * 2**20
         ),
         cost_estimate=pl.CostEstimate(
             flops=32 * rows * rows * width, bytes_accessed=12 * rows * width, transcendentals=8 * rows * rows

time: 177 us -> 176 us (level)
  local copies, waits for them, and re-layouts: 2.82 us -> 0 us
    unnamed x6 -> x0, local copies, waits for them, and re-layouts: 2.82 us -> none
where the time goes in v3:
time: 176 us
  Pallas kernels  170 us (97%)
  other arithmetic  3.18 us (2%)
  between operations  1.93 us (1%)
    pallas_call x1, Pallas kernels, body(): pl.pallas_call(kernel, out_shape=(total, total), in_specs=[hbm, hbm, hbm,...  170 us

profile of v3, /device:TPU:1, one launch (start us, length us, event | category | flops | bytes accessed | tf_op | source)
XLA Modules:
  0.0 175.5 jit_solution(14166793843333483798)
XLA Ops:
  1.9 170.4 %shard_map.68 = (f32[256,1152]{1,0:T(8,128)}, f32[256,1152]{1,0:T(8,128)}) custom-call(bf16[256,1152]{1,0:T(8,128)(2,1)} %photo.1, bf16[256,1152]{1,0:T(8,128)(2,1)} %text.1, s32[16,64]{1,0:T(8,128)} %bitcast.5, f32[1]{0:T(128)} %bitcast.3.factor, f32[1]{0:T(128)} %bitcast.4.bias), custom_call_target="tpu_custom_call" | custom-call | flops 2415919104 | bytes 3538944 | tf_op jit(solution)/shard_map/pallas_call | solution.py:341
  172.4 3.2 %broadcast_multiply_fusion = (f32[256,1152]{1,0:T(8,128)}, f32[256,1152]{1,0:T(8,128)}) fusion(f32[256,1152]{1,0:T(8,128)} %get-tuple-element.5, f32[]{:T(128)} %copy.7, f32[256,1152]{1,0:T(8,128)} %get-tuple-element.4), kind=kLoop, calls=%fused_computation | loop fusion | flops 589824 | bytes 4718596 | tf_op jit(solution)/shard_map/mul | solution.py:375

commit v4 on v3

--- a/solution.py
+++ b/solution.py
@@ -15,7 +15,7 @@
 K0 = HALF + STEPS - 1
 SLOTS = K0 + STEPS
 LAST = HALF - 1
-PARTS = 4
+PARTS = 8
 
 
 def device(x, y, z, core):

time: 176 us -> 176 us (level)
  no operation moved by 1% of the time
where the time goes in v4:
time: 176 us
  Pallas kernels  170 us (97%)
  other arithmetic  3.18 us (2%)
  between operations  1.93 us (1%)
    pallas_call x1, Pallas kernels, body(): pl.pallas_call(kernel, out_shape=(total, total), in_specs=[hbm, hbm, hbm,...  170 us

profile of v4, /device:TPU:1, one launch (start us, length us, event | category | flops | bytes accessed | tf_op | source)
XLA Modules:
  0.0 175.6 jit_solution(965764499647431160)
XLA Ops:
  1.9 170.5 %shard_map.68 = (f32[256,1152]{1,0:T(8,128)}, f32[256,1152]{1,0:T(8,128)}) custom-call(bf16[256,1152]{1,0:T(8,128)(2,1)} %photo.1, bf16[256,1152]{1,0:T(8,128)(2,1)} %text.1, s32[16,64]{1,0:T(8,128)} %bitcast.5, f32[1]{0:T(128)} %bitcast.3.factor, f32[1]{0:T(128)} %bitcast.4.bias), custom_call_target="tpu_custom_call" | custom-call | flops 2415919104 | bytes 3538944 | tf_op jit(solution)/shard_map/pallas_call | solution.py:341
  172.4 3.2 %broadcast_multiply_fusion = (f32[256,1152]{1,0:T(8,128)}, f32[256,1152]{1,0:T(8,128)}) fusion(f32[256,1152]{1,0:T(8,128)} %get-tuple-element.5, f32[]{:T(128)} %copy.7, f32[256,1152]{1,0:T(8,128)} %get-tuple-element.4), kind=kLoop, calls=%fused_computation | loop fusion | flops 589824 | bytes 4718596 | tf_op jit(solution)/shard_map/mul | solution.py:375
